TPU v7x, 256 devices: a whole 4x4x8 slice. The times are simulated.
256 devices in a mesh: pair: 32 (over z, y), cd: 8 (over x, core).
Axes of the slice: x: 4, y: 4, z: 8, core: 2. Of those that a mesh axis runs over, the one named last changes fastest.
Arguments:
- amplitudes: bfloat16 [8192, 4096], P('pair', 'cd'), may hold values from -6 to 6
- integrals: bfloat16 [2, 8192, 4096], P(None, 'pair', 'cd'), may hold values from -0.1875 to 0.1875
- row_irreps: int32 [32, 2], P('pair'), may hold values from 0 to 3
- col_irreps: int32 [16, 2], P('cd'), may hold values from 0 to 3
Outputs:
- sigma: bfloat16 [8192, 8192], P('cd', 'pair')
All inputs are finite; a program needn't handle non-finite values.
Results may differ from a plain program's by a relative error of at most 0.014.
Values may be sent and summed in bfloat16 or wider, within the bound.
A program may use at most 192 MiB of HBM per device.

v0:
```python
import jax
import jax.numpy as jnp
from jax import lax
from jax.sharding import PartitionSpec as P


def pair_symmetry(labels):
    return jnp.bitwise_xor(labels[:, 0], labels[:, 1])


def tile_product(left_part, right_part):
    return lax.dot_general(
        left_part, right_part, (((1,), (1,)), ((), ())), preferred_element_type=jnp.float32
    )


def on_device(amplitudes, integrals, row_irreps, col_irreps):
    row_tiles = row_irreps.shape[0]
    col_tiles = col_irreps.shape[0]
    tile_size = integrals.shape[1] // row_tiles
    allowed = pair_symmetry(row_irreps)[:, None] == pair_symmetry(col_irreps)[None, :]
    raw_rows = lax.all_gather(amplitudes, "pair", axis=0, tiled=True)
    middle = raw_rows.shape[0] // 2
    direct = raw_rows[:middle].astype(jnp.float32)
    mirrored = raw_rows[middle:].astype(jnp.float32)
    gathered = jnp.concatenate([direct + mirrored, direct - mirrored], 0).astype(jnp.bfloat16)
    half_rows = gathered.shape[0] // 2
    shard_rows = gathered.shape[0] // lax.axis_size("cd")
    weight_mask = allowed.astype(jnp.bfloat16)
    shaped = (
        integrals.reshape(2, row_tiles, tile_size, col_tiles, tile_size)
        * weight_mask[None, :, None, :, None]
    )
    weights = shaped.reshape(integrals.shape)

    def contract(row_block, channel_weights):
        return tile_product(row_block, channel_weights)

    first_index = jnp.int32(0)
    pieces = []
    for number in range(shard_rows * lax.axis_size("cd") // shard_rows):
        first_row = first_index + number * shard_rows
        upper = (first_row >= half_rows).astype(jnp.int32)
        local_row = first_row - upper * half_rows
        plus_rows = lax.dynamic_slice_in_dim(gathered, local_row, shard_rows, 0)
        minus_rows = lax.dynamic_slice_in_dim(gathered, local_row + half_rows, shard_rows, 0)
        plus_term = contract(plus_rows, weights[0])
        minus_term = contract(minus_rows, weights[1])
        factor = 1.0 - 2.0 * upper.astype(jnp.float32)
        pieces.append(plus_term + factor * minus_term)
    return lax.psum_scatter(
        jnp.concatenate(pieces, 0).astype(jnp.bfloat16), "cd", scatter_dimension=0, tiled=True
    )


def solution(mesh):
    in_specs = (P("pair", "cd"), P(None, "pair", "cd"), P("pair", None), P("cd", None))
    out_specs = P("cd", "pair")
    return jax.shard_map(
        on_device, mesh=mesh, in_specs=in_specs, out_specs=out_specs, check_vma=False
    )
```

profile of v0, /device:TPU:32, one launch (start us, length us, event | category | flops | bytes accessed | tf_op | source)
XLA Modules:
  0.0 170.9 jit_solution(2034880087262283231)
XLA Ops:
  6.5 0.0 all-gather.2.cloned.1.call-start
  6.5 0.7 all-gather.2.cloned.1.call-update
  7.3 0.0 reduce-scatter.2.cloned.1.call-start
  7.3 1.2 reshape.47
  8.5 1.3 fusion.28
  11.1 0.9 fusion.26
  12.1 0.5 broadcast_multiply_fusion
  12.6 0.4 fusion.27
  13.0 96.3 %all-gather.2.cloned.1.call-done = bf16[8192,512]{1,0:T(8,128)(2,1)} async-done(((bf16[256,512]{1,0:T(8,128)(2,1)}), bf16[8192,512]{1,0:T(8,128)(2,1)}) %all-gather.2.cloned.1.call-update) | async-done | bytes 8388624 | tf_op jit(solution)/shard_map/all_gather | solution.py:22
  109.4 4.4 %fusion.1 = (bf16[4096,512]{1,0:T(8,128)(2,1)S(1)}, bf16[4096,512]{1,0:T(8,128)(2,1)S(1)}) fusion(bf16[8192,512]{1,0:T(8,128)(2,1)} %all-gather.2.cloned.1.call-done), kind=kLoop, calls=%fused_computation.3 | loop fusion | flops 12582912 | bytes 16777216 | tf_op jit(solution)/shard_map/convert.10
  113.8 0.5 fusion.2
  114.3 0.5 fusion.6
  114.7 0.5 fusion.10
  115.2 0.5 fusion.14
  115.7 1.3 fusion.18
  116.9 1.3 fusion.19
  118.2 1.3 fusion.20
  119.5 1.3 fusion.21
  120.8 0.9 fusion.22
  121.7 1.0 fusion.23
  122.7 0.9 fusion.24
  123.6 0.9 fusion.25
  124.5 0.0 reduce-scatter.2.cloned.1.call-update
  124.6 39.5 %reduce-scatter.2.cloned.1.call-done = bf16[1024,256]{1,0:T(8,128)(2,1)} async-done(((bf16[8192,256]{1,0:T(8,128)(2,1)}), bf16[1024,256]{1,0:T(8,128)(2,1)}) %reduce-scatter.2.cloned.1.call-update) | async-done | bytes 524304 | tf_op jit(solution)/shard_map/reduce_scatter | solution.py:51
  (2 shorter events, 0.1 us)
Async XLA Ops:
  6.5 102.8 %all-gather.2.cloned.1.call-start = ((), (), s32[]{:S(2)}) async-start(), calls=%async_computation.1 | async-start | bytes 8650752 | tf_op jit(solution)/shard_map/all_gather | solution.py:22
  7.3 156.8 %reduce-scatter.2.cloned.1.call-start = ((), (), s32[]{:S(2)}) async-start(), calls=%async_computation.2 | async-start | bytes 4718592 | tf_op jit(solution)/shard_map/reduce_scatter | solution.py:51
Sparse Core Ops, SparseCore 0:
  9.9 99.3 all-gather.1
  124.7 39.3 reduce-scatter.1
where the time goes:
time: 171 us
  waiting for transfers between devices  137 us (80%)
  between operations  14.8 us (9%)
  other arithmetic  9.62 us (6%)
  matrix products  6.97 us (4%)
  local copies, waits for them, and re-layouts  2.91 us (2%)
    all_gather x1, waiting for transfers between devices, on_device(): raw_rows = lax.all_gather(amplitudes, 'pair', axis=0, tiled=True)  96.3 us
    reduce_scatter x1, waiting for transfers between devices, on_device(): lax.psum_scatter(jnp.concatenate(pieces, 0).astype(jnp.bfloat16), 'cd', s...  39.5 us
    dot_general x8, matrix products, tile_product(): lax.dot_general(left_part, right_part, (((1,), (1,)), ((), ())), preferre...  6.97 us
    another operation x1, other arithmetic  4.4 us
  transfers between devices with their start and end apart: 2, of which 2 were waited for; matrix products, arithmetic and copies ran while one was open for 3% of the time, Pallas kernels for 0%

commit v1 on v0

v1 whole, which is shorter than its diff:
```python
import functools

import jax
import jax.numpy as jnp
from jax import lax
from jax.experimental import pallas as pl
from jax.experimental.pallas import tpu as pltpu
from jax.sharding import PartitionSpec as P

MESH = pl.DeviceIdType.MESH
NX, NY, NZ = 4, 4, 8

CHUNKS = (64, 64, 64, 64)

STEPS = None


def coordinates():
    pair, cd = lax.axis_index("pair"), lax.axis_index("cd")
    return lax.div(cd, 2), lax.rem(pair, NY), lax.div(pair, NY), lax.rem(cd, 2)


def kernel(
    steps, amp, integ, row_ir, col_ir, out,
    ag, asib, pk, wb, cp, sx1, rx1, sx2, rx2, res,
    loc, zs, zr, ds, dr, ys, yr, ws, wr, x1s, x1r, x2s, x2r, os, orr,
):
    x, y, z, c = coordinates()
    sib = 1 - c
    chunks = CHUNKS
    starts = [sum(chunks[:k]) for k in range(len(chunks))]
    tiles = {}
    offset = 0
    for r, n in enumerate(chunks):
        for g in range(4):
            tiles[r, g] = (len(tiles), offset)
            offset += n

    def dev(dx=0, dy=0, dz=0, flip=False):
        return (
            lax.rem(z + dz + NZ, NZ) * NY + lax.rem(y + dy + NY, NY),
            lax.rem(x + dx + NX, NX) * 2 + (sib if flip else c),
        )

    load_a = pltpu.make_async_copy(amp, ag.at[z], loc.at[0])
    load_w = pltpu.make_async_copy(integ, wb.at[0, :, :, pl.ds(0, 512)], loc.at[1])
    load_a.start()
    load_w.start()
    barrier = pltpu.get_barrier_semaphore()
    partners = [
        dev(dx=1), dev(dx=-1), dev(dy=1), dev(dy=-1), dev(dy=2), dev(dz=1), dev(dz=-1), dev(flip=True),
    ]
    for partner in partners:
        pl.semaphore_signal(barrier, inc=1, device_id=partner, device_id_type=MESH)
    started = []

    def remote(src, dst, send, recv, to):
        return pltpu.make_async_remote_copy(
            src_ref=src, dst_ref=dst, send_sem=send, recv_sem=recv, device_id=to, device_id_type=MESH
        )

    def go(copy):
        copy.start()
        started.append(copy)

    def z_rows(r, s, d):
        if d < 4:
            return pl.ds(starts[r], chunks[r])
        half = chunks[r] // 2
        return pl.ds(starts[r] + (0 if s == 0 else half), half)

    def z_copy(r, s, d, behind):
        sign = 1 if s == 0 else -1
        block = ag.at[lax.rem(z - sign * behind + NZ, NZ), z_rows(r, s, d)]
        return remote(block, block, zs.at[r, s, d - 1], zr.at[r, s, d - 1], dev(dz=sign))

    def z_send(r, d):
        for s in (0, 1):
            go(z_copy(r, s, d, d - 1))

    def z_wait(r, d):
        for s in (0, 1):
            z_copy(r, s, d, d).wait_recv()

    def y_half(s, n):
        return s if n != 1 else 1 - s

    def y_copy(s, n):
        sign = 1 if s == 0 else -1
        half = pl.ds(128 * y_half(s, n), 128)
        src = wb.at[0 if n < 2 else 1, :, half, pl.ds(0, 512)]
        dst = wb.at[n + 1, :, half, pl.ds(0, 512)]
        return remote(src, dst, ys.at[s, n], yr.at[s, n], dev(dy=sign))

    def w_give(g):
        return remote(
            wb.at[g, :, :, pl.ds(0, 512)], wb.at[g, :, :, pl.ds(512, 512)], ws.at[g], wr.at[g], dev(flip=True)
        )

    def a_give(r):
        rows = pl.ds(starts[r], chunks[r])
        src = ag.reshape(4, 2, 256, 512).at[:, sib, rows]
        return remote(src, asib.at[:, rows], ds.at[r], dr.at[r], dev(flip=True))

    def x1_copy(r, g, s):
        t, off = tiles[r, g]
        half = chunks[r] // 2
        rows = pl.ds(off + s * half, half)
        return remote(
            sx1.at[rows], rx1.at[rows], x1s.at[t, s], x1r.at[t, s], dev(dx=1 if s == 0 else -1)
        )

    def x2_copy(r, g, s):
        t, off = tiles[r, g]
        rows = pl.ds(off, chunks[r])
        return remote(
            sx2.at[s, rows], rx2.at[s, rows], x2s.at[t, s], x2r.at[t, s], dev(dx=1 if s == 0 else -1)
        )

    def owner(g, h):
        return {1: (-1, 1), 2: (1, -1), 3: (2, 2)}[g][h]

    def o_copy(r, g, h, origin, to):
        t, off = tiles[r, g]
        cols = pl.ds(128 * h, 128)
        dst = out.at[pl.ds(pl.multiple_of(origin * 256 + starts[r], 32), chunks[r]), cols]
        return remote(res.at[pl.ds(off, chunks[r]), cols], dst, os.at[t, h], orr.at[t, h], to)

    def multiply(r, g):
        t, off = tiles[r, g]
        n = chunks[r]
        rows = pl.ds(2 * starts[r], 2 * n)
        dims = (((1,), (1,)), ((), ()))
        plus = lax.dot_general(pk[0, rows], wb[g, 0], dims, preferred_element_type=jnp.float32)
        minus = lax.dot_general(pk[1, rows], wb[g, 1], dims, preferred_element_type=jnp.float32)
        upper, lower = plus + minus, plus - minus
        own = pl.ds(off, n)
        cp[0, own] = upper[:n]
        cp[1, own] = upper[n:]
        cp[2, own] = lower[:n]
        cp[3, own] = lower[n:]
        sx1[own] = cp[lax.rem(x + 2, NX), own].astype(jnp.bfloat16)
        for s in (0, 1):
            go(x1_copy(r, g, s))

    def add_on(r, g):
        t, off = tiles[r, g]
        n = chunks[r]
        half = n // 2
        for s in (0, 1):
            x1_copy(r, g, s).wait_recv()
            target = lax.rem(x + (1 if s == 0 else 3), NX)
            for k in (0, 1):
                part = pl.ds(off + k * half, half)
                value = cp[target, part]
                if k == s:
                    value = value + rx1[part].astype(jnp.float32)
                sx2[s, part] = value.astype(jnp.bfloat16)
            go(x2_copy(r, g, s))

    def finish(r, g):
        t, off = tiles[r, g]
        n = chunks[r]
        own = pl.ds(off, n)
        for s in (0, 1):
            x2_copy(r, g, s).wait_recv()
        total = cp[x, own] + rx2[0, own].astype(jnp.float32) + rx2[1, own].astype(jnp.float32)
        total = total.astype(jnp.bfloat16)
        if g == 0:
            out[pl.ds(pl.multiple_of(y * 256 + starts[r], 32), n)] = total
        else:
            res[own] = total
            for h in (0, 1):
                go(o_copy(r, g, h, y, dev(dy=owner(g, h))))

    def pack(r):
        a_give(r).wait_recv()
        n = chunks[r]
        rows = pl.ds(starts[r], n)
        for i in (0, 1):
            to = pl.ds(2 * starts[r] + i * n, n)
            for k, (direct, mirror) in enumerate((
                (ag[c + 2 * i, rows], ag[c + 2 * i + 4, rows]),
                (asib[i, rows], asib[i + 2, rows]),
            )):
                direct, mirror = direct.astype(jnp.float32), mirror.astype(jnp.float32)
                cols = pl.ds(512 * k, 512)
                pk[0, to, cols] = (direct + mirror).astype(jnp.bfloat16)
                pk[1, to, cols] = (direct - mirror).astype(jnp.bfloat16)

    load_a.wait()
    load_w.wait()
    row_sym = row_ir[0, 0] ^ row_ir[0, 1]
    for k in (0, 1):
        keep = (row_sym == (col_ir[k, 0] ^ col_ir[k, 1])).astype(jnp.int32).astype(jnp.float32)
        cols = pl.ds(256 * k, 256)
        for s in (0, 1):
            wb[0, s, :, cols] = (wb[0, s, :, cols].astype(jnp.float32) * keep).astype(jnp.bfloat16)
    pl.semaphore_wait(barrier, len(partners))

    for step in steps:
        name, args = step[0], step[1:]
        if name == "zo":
            z_send(args[0], 1)
        elif name == "zf":
            z_wait(*args)
            z_send(args[0], args[1] + 1)
        elif name == "zc":
            z_wait(args[0], 4)
            go(a_give(args[0]))
        elif name == "pk":
            pack(*args)
        elif name == "wo":
            for s in (0, 1):
                go(y_copy(s, args[0]))
        elif name == "wg":
            go(w_give(0))
        elif name == "wf":
            for s in (0, 1):
                y_copy(s, args[0]).wait_recv()
            if args[0] == 0:
                for s in (0, 1):
                    go(y_copy(s, 2))
            go(w_give(args[0] + 1))
        elif name == "ws":
            w_give(args[0]).wait_recv()
        elif name == "mm":
            multiply(*args)
        elif name == "ra":
            add_on(*args)
        elif name == "fi":
            finish(*args)
    for r in range(len(chunks)):
        for g in (1, 2, 3):
            for h in (0, 1):
                back = owner(g, h)
                origin = lax.rem(y - back + NY, NY)
                o_copy(r, g, h, origin, dev(dy=back)).wait_recv()
    for copy in started:
        copy.wait_send()


STEPS = [
    ("zo", 0), ("wo", 0), ("zo", 1), ("wg",), ("wo", 1), ("zf", 0, 1), ("zo", 2), ("zf", 0, 2), ("zf", 1, 1),
    ("wf", 0), ("zf", 0, 3), ("zo", 3), ("ws", 0), ("zc", 0), ("zf", 1, 2), ("ws", 1), ("pk", 0), ("mm", 0, 0), ("zf", 2, 1),
    ("mm", 0, 1), ("zf", 1, 3), ("ra", 0, 0), ("wf", 1), ("ra", 0, 1), ("fi", 0, 0), ("zf", 2, 2), ("fi", 0, 1),
    ("zc", 1), ("ws", 2), ("mm", 0, 2), ("zf", 3, 1), ("pk", 1), ("mm", 1, 0), ("ra", 0, 2), ("zf", 2, 3), ("mm", 1, 1),
    ("ra", 1, 0), ("fi", 0, 2), ("mm", 1, 2), ("zf", 3, 2), ("ra", 1, 1), ("zc", 2), ("fi", 1, 0), ("ra", 1, 2), ("wf", 2), ("fi", 1, 1),
    ("pk", 2), ("mm", 2, 0), ("fi", 1, 2), ("zf", 3, 3), ("mm", 2, 1), ("ws", 3), ("ra", 2, 0), ("mm", 2, 2), ("ra", 2, 1), ("fi", 2, 0),
    ("mm", 0, 3), ("ra", 2, 2), ("zc", 3), ("fi", 2, 1), ("mm", 1, 3), ("ra", 0, 3), ("fi", 2, 2), ("mm", 2, 3), ("ra", 1, 3), ("fi", 0, 3),
    ("pk", 3), ("mm", 3, 0), ("ra", 2, 3), ("fi", 1, 3), ("mm", 3, 1), ("ra", 3, 0), ("fi", 2, 3), ("mm", 3, 2), ("ra", 3, 1), ("fi", 3, 0),
    ("mm", 3, 3), ("ra", 3, 2), ("fi", 3, 1), ("ra", 3, 3), ("fi", 3, 2), ("fi", 3, 3),
]


def on_device(amplitudes, integrals, row_irreps, col_irreps):
    count, bf16, dma = len(CHUNKS), jnp.bfloat16, pltpu.SemaphoreType.DMA
    any_space, smem, vmem = (pl.BlockSpec(memory_space=s) for s in (pl.ANY, pltpu.SMEM, pltpu.VMEM))
    return pl.pallas_call(
        functools.partial(kernel, STEPS),
        out_shape=jax.ShapeDtypeStruct((1024, 256), bf16),
        in_specs=[any_space, any_space, smem, smem],
        out_specs=vmem,
        scratch_shapes=[
            pltpu.VMEM((8, 256, 512), bf16),
            pltpu.VMEM((4, 256, 512), bf16),
            pltpu.VMEM((2, 512, 1024), bf16),
            pltpu.VMEM((4, 2, 256, 1024), bf16),
            pltpu.VMEM((4, 1024, 256), jnp.float32),
            pltpu.VMEM((1024, 256), bf16),
            pltpu.VMEM((1024, 256), bf16),
            pltpu.VMEM((2, 1024, 256), bf16),
            pltpu.VMEM((2, 1024, 256), bf16),
            pltpu.VMEM((1024, 256), bf16),
            dma((2,)),
            dma((count, 2, 4)), dma((count, 2, 4)),
            dma((count,)), dma((count,)),
            dma((2, 3)), dma((2, 3)),
            dma((4,)), dma((4,)),
            dma((4 * count, 2)), dma((4 * count, 2)),
            dma((4 * count, 2)), dma((4 * count, 2)),
            dma((4 * count, 2)), dma((4 * count, 2)),
        ],
        compiler_params=pltpu.CompilerParams(
            collective_id=0, has_side_effects=True, vmem_limit_bytes=48 * 2**20
        ),
        cost_estimate=pl.CostEstimate(flops=2 * 2**30, bytes_accessed=2 * 2**20, transcendentals=0),
        name="ladder",
    )(amplitudes, integrals, row_irreps, col_irreps)


def solution(mesh):
    in_specs = (P("pair", "cd"), P(None, "pair", "cd"), P("pair", None), P("cd", None))
    out_specs = P("cd", "pair")
    return jax.shard_map(
        on_device, mesh=mesh, in_specs=in_specs, out_specs=out_specs, check_vma=False
    )
```

time: 171 us -> 84.3 us (0.49)
  waiting for transfers between devices: 137 us -> 0 us
  Pallas kernels: 0 us -> 79.2 us
  between operations: 14.8 us -> 0.01 us
  other arithmetic: 9.62 us -> 0 us
  matrix products: 6.97 us -> 0 us
    all_gather x1 -> x0, waiting for transfers between devices: 96.3 us -> none  [on_device(): raw_rows = lax.all_gather(amplitudes, 'pair', axis=0, tiled=True)]
    pallas_call x0 -> x1, Pallas kernels: none -> 79.2 us  [on_device(): pl.pallas_call(functools.partial(kernel, STEPS), out_shape=jax.ShapeDtype...]
    reduce_scatter x1 -> x0, waiting for transfers between devices: 39.5 us -> none  [on_device(): lax.psum_scatter(jnp.concatenate(pieces, 0).astype(jnp.bfloat16), 'cd', s...]
    dot_general x8 -> x0, matrix products: 6.97 us -> none  [tile_product(): lax.dot_general(left_part, right_part, (((1,), (1,)), ((), ())), preferre...]
    another operation x1 -> x0, other arithmetic: 4.4 us -> none
    unnamed x2 -> x9, local copies, waits for them, and re-layouts: 0.06 us -> 4.12 us
    unnamed x3 -> x0, other arithmetic: 2.83 us -> none
  transfers between devices with their start and end apart: 2 -> 0, of which waited for: 2 -> 0; matrix products, arithmetic and copies ran while one was open for 3% -> 0% of each run, Pallas kernels for 0% -> 0%
where the time goes in v1:
time: 84.3 us; the launch traced here: 83.4 us
  Pallas kernels  79.2 us (94%)
  local copies, waits for them, and re-layouts  4.12 us (5%)
    pallas_call x1, Pallas kernels, on_device(): pl.pallas_call(functools.partial(kernel, STEPS), out_shape=jax.ShapeDtype...  79.2 us
    unnamed x9, local copies, waits for them, and re-layouts  4.12 us

profile of v1, /device:TPU:32, one launch (start us, length us, event | category | flops | bytes accessed | tf_op | source)
XLA Modules:
  0.0 83.4 jit_solution(8638729383388107467)
XLA Ops:
  0.0 0.0 copy-start
  0.0 1.0 %copy-done = bf16[2,256,512]{2,1,0:T(8,128)(2,1)S(1)} copy-done((bf16[2,256,512]{2,1,0:T(8,128)(2,1)S(1)}, bf16[2,256,512]{2,1,0:T(8,128)(2,1)}, u32[]{:S(2)}) %copy-start) | copy-done | bytes 524312
  1.0 0.0 copy-start.1
  1.0 0.9 %copy-done.1 = bf16[256,512]{1,0:T(8,128)(2,1)S(1)} copy-done((bf16[256,512]{1,0:T(8,128)(2,1)S(1)}, bf16[256,512]{1,0:T(8,128)(2,1)}, u32[]{:S(2)}) %copy-start.1) | copy-done | bytes 262168
  2.0 0.0 copy-start.2
  2.0 0.7 copy-done.2
  2.7 0.0 copy-start.3
  2.7 0.7 copy-done.3
  3.3 79.2 %ladder.1 = bf16[1024,256]{1,0:T(8,128)(2,1)S(1)} custom-call(bf16[256,512]{1,0:T(8,128)(2,1)S(1)} %copy-done.1, bf16[2,256,512]{2,1,0:T(8,128)(2,1)S(1)} %copy-done, s32[1,2]{1,0:T(1,128)S(1)} %copy-done.3, s32[2,2]{1,0:T(2,128)S(1)} %copy-done.2), custom_call_target="tpu_custom_call" | custom-call | flops 2147483648 | bytes 2097152 | tf_op jit(solution)/shard_map/ladder/pallas_call | solution.py:259
  82.6 0.8 copy.6
Async XLA Ops:
  0.0 1.0 %copy-start = (bf16[2,256,512]{2,1,0:T(8,128)(2,1)S(1)}, bf16[2,256,512]{2,1,0:T(8,128)(2,1)}, u32[]{:S(2)}) copy-start(bf16[2,256,512]{2,1,0:T(8,128)(2,1)} %integ.1) | copy-start | bytes 1572868
  1.0 0.9 %copy-start.1 = (bf16[256,512]{1,0:T(8,128)(2,1)S(1)}, bf16[256,512]{1,0:T(8,128)(2,1)}, u32[]{:S(2)}) copy-start(bf16[256,512]{1,0:T(8,128)(2,1)} %amp.1) | copy-start | bytes 786436
  2.0 0.7 copy-start.2
  2.7 0.7 copy-start.3

commit v2 on v1

--- a/solution.py
+++ b/solution.py
@@ -21,9 +21,9 @@
 
 
 def kernel(
-    steps, amp, integ, row_ir, col_ir, out,
+    steps, amp, integ, row_hbm, col_hbm, out, row_ir, col_ir,
     ag, asib, pk, wb, cp, sx1, rx1, sx2, rx2, res,
-    loc, zs, zr, ds, dr, ys, yr, ws, wr, x1s, x1r, x2s, x2r, os, orr,
+    loc, zs, zr, zq, ds, dr, ys, yr, ws, wr, x1s, x1r, x2s, x2r, os, orr,
 ):
     x, y, z, c = coordinates()
     sib = 1 - c
@@ -44,8 +44,13 @@
 
     load_a = pltpu.make_async_copy(amp, ag.at[z], loc.at[0])
     load_w = pltpu.make_async_copy(integ, wb.at[0, :, :, pl.ds(0, 512)], loc.at[1])
-    load_a.start()
-    load_w.start()
+    loads = [
+        load_w, load_a,
+        pltpu.make_async_copy(row_hbm, row_ir, loc.at[2]),
+        pltpu.make_async_copy(col_hbm, col_ir, loc.at[3]),
+    ]
+    for load in loads:
+        load.start()
     barrier = pltpu.get_barrier_semaphore()
     partners = [
         dev(dx=1), dev(dx=-1), dev(dy=1), dev(dy=-1), dev(dy=2), dev(dz=1), dev(dz=-1), dev(flip=True),
@@ -63,6 +68,8 @@
         copy.start()
         started.append(copy)
 
+    mine = lax.rem(z, 2) == c
+
     def z_rows(r, s, d):
         if d < 4:
             return pl.ds(starts[r], chunks[r])
@@ -74,13 +81,41 @@
         block = ag.at[lax.rem(z - sign * behind + NZ, NZ), z_rows(r, s, d)]
         return remote(block, block, zs.at[r, s, d - 1], zr.at[r, s, d - 1], dev(dz=sign))
 
+    def cross_copy(r, s, behind):
+        sign = 1 if s == 0 else -1
+        origin = lax.rem(z - sign * behind + NZ, NZ)
+        rows = z_rows(r, s, 4)
+        return remote(
+            ag.at[origin, rows], asib.at[lax.div(origin, 2), rows], zs.at[r, s, 3], zq.at[r, s], dev(dz=sign, flip=True)
+        )
+
     def z_send(r, d):
         for s in (0, 1):
-            go(z_copy(r, s, d, d - 1))
+            copy = z_copy(r, s, d, d - 1)
+            if d < 4:
+                go(copy)
+            else:
+                pl.when(jnp.logical_not(mine))(copy.start)
+                pl.when(mine)(cross_copy(r, s, 3).start)
+                started.append(copy)
 
     def z_wait(r, d):
         for s in (0, 1):
             z_copy(r, s, d, d).wait_recv()
+
+    def share(r, e, far):
+        origin = lax.rem(z + far + NZ, NZ)
+        rows = pl.ds(starts[r], chunks[r])
+        return remote(
+            ag.at[origin, rows], asib.at[lax.div(origin, 2), rows], ds.at[r, e], dr.at[r, e], dev(flip=True)
+        )
+
+    def give(r, d):
+        sends = {0: ((2, 0),), 1: ((0, 1), (1, -1)), 2: ((0, 2), (1, -2)), 3: ((2, 3), (3, -3))}[d]
+        def act():
+            for e, far in sends:
+                share(r, e, far).start()
+        pl.when(mine if d % 2 else jnp.logical_not(mine))(act)
 
     def y_half(s, n):
         return s if n != 1 else 1 - s
@@ -97,22 +132,16 @@
             wb.at[g, :, :, pl.ds(0, 512)], wb.at[g, :, :, pl.ds(512, 512)], ws.at[g], wr.at[g], dev(flip=True)
         )
 
-    def a_give(r):
-        rows = pl.ds(starts[r], chunks[r])
-        src = ag.reshape(4, 2, 256, 512).at[:, sib, rows]
-        return remote(src, asib.at[:, rows], ds.at[r], dr.at[r], dev(flip=True))
-
     def x1_copy(r, g, s):
         t, off = tiles[r, g]
-        half = chunks[r] // 2
-        rows = pl.ds(off + s * half, half)
-        return remote(
-            sx1.at[rows], rx1.at[rows], x1s.at[t, s], x1r.at[t, s], dev(dx=1 if s == 0 else -1)
+        rows = pl.ds(off, chunks[r])
+        return remote(
+            sx1.at[s, rows], rx1.at[s, rows], x1s.at[t, s], x1r.at[t, s], dev(dx=1 if s == 0 else -1)
         )
 
     def x2_copy(r, g, s):
         t, off = tiles[r, g]
-        rows = pl.ds(off, chunks[r])
+        rows = pl.ds(off // 2, chunks[r] // 2)
         return remote(
             sx2.at[s, rows], rx2.at[s, rows], x2s.at[t, s], x2r.at[t, s], dev(dx=1 if s == 0 else -1)
         )
@@ -139,42 +168,52 @@
         cp[1, own] = upper[n:]
         cp[2, own] = lower[:n]
         cp[3, own] = lower[n:]
-        sx1[own] = cp[lax.rem(x + 2, NX), own].astype(jnp.bfloat16)
-        for s in (0, 1):
+        half = n // 2
+        for s in (0, 1):
+            target = lax.rem(x + (1 if s == 0 else 3), NX)
+            sx1[s, pl.ds(off, half)] = cp[lax.rem(x + 2, NX), pl.ds(off + s * half, half)].astype(jnp.bfloat16)
+            sx1[s, pl.ds(off + half, half)] = cp[target, pl.ds(off + (1 - s) * half, half)].astype(jnp.bfloat16)
             go(x1_copy(r, g, s))
 
     def add_on(r, g):
+        t, off = tiles[r, g]
+        half = chunks[r] // 2
+        for s in (0, 1):
+            x1_copy(r, g, s).wait_recv()
+            target = lax.rem(x + (1 if s == 0 else 3), NX)
+            value = cp[target, pl.ds(off + s * half, half)] + rx1[s, pl.ds(off, half)].astype(jnp.float32)
+            sx2[s, pl.ds(off // 2, half)] = value.astype(jnp.bfloat16)
+            go(x2_copy(r, g, s))
+
+    def finish(r, g):
         t, off = tiles[r, g]
         n = chunks[r]
         half = n // 2
         for s in (0, 1):
-            x1_copy(r, g, s).wait_recv()
-            target = lax.rem(x + (1 if s == 0 else 3), NX)
-            for k in (0, 1):
-                part = pl.ds(off + k * half, half)
-                value = cp[target, part]
-                if k == s:
-                    value = value + rx1[part].astype(jnp.float32)
-                sx2[s, part] = value.astype(jnp.bfloat16)
-            go(x2_copy(r, g, s))
-
-    def finish(r, g):
-        t, off = tiles[r, g]
-        n = chunks[r]
-        own = pl.ds(off, n)
-        for s in (0, 1):
             x2_copy(r, g, s).wait_recv()
-        total = cp[x, own] + rx2[0, own].astype(jnp.float32) + rx2[1, own].astype(jnp.float32)
-        total = total.astype(jnp.bfloat16)
-        if g == 0:
-            out[pl.ds(pl.multiple_of(y * 256 + starts[r], 32), n)] = total
-        else:
-            res[own] = total
+        for s in (0, 1):
+            total = (
+                cp[x, pl.ds(off + s * half, half)]
+                + rx2[s, pl.ds(off // 2, half)].astype(jnp.float32)
+                + rx1[1 - s, pl.ds(off + half, half)].astype(jnp.float32)
+            ).astype(jnp.bfloat16)
+            if g == 0:
+                out[pl.ds(pl.multiple_of(y * 256 + starts[r] + s * half, 16), half)] = total
+            else:
+                res[pl.ds(off + s * half, half)] = total
+        if g > 0:
             for h in (0, 1):
                 go(o_copy(r, g, h, y, dev(dy=owner(g, h))))
 
     def pack(r):
-        a_give(r).wait_recv()
+        for e in (0, 1, 2):
+            share(r, e, 0).wait_recv()
+        pl.when(jnp.logical_not(mine))(share(r, 3, 0).wait_recv)
+        def last_hop():
+            for s in (0, 1):
+                z_copy(r, s, 4, 4).wait_recv()
+                cross_copy(r, s, 4).wait_recv()
+        pl.when(mine)(last_hop)
         n = chunks[r]
         rows = pl.ds(starts[r], n)
         for i in (0, 1):
@@ -188,8 +227,8 @@
                 pk[0, to, cols] = (direct + mirror).astype(jnp.bfloat16)
                 pk[1, to, cols] = (direct - mirror).astype(jnp.bfloat16)
 
-    load_a.wait()
-    load_w.wait()
+    for load in loads:
+        load.wait()
     row_sym = row_ir[0, 0] ^ row_ir[0, 1]
     for k in (0, 1):
         keep = (row_sym == (col_ir[k, 0] ^ col_ir[k, 1])).astype(jnp.int32).astype(jnp.float32)
@@ -202,12 +241,11 @@
         name, args = step[0], step[1:]
         if name == "zo":
             z_send(args[0], 1)
+            give(args[0], 0)
         elif name == "zf":
             z_wait(*args)
             z_send(args[0], args[1] + 1)
-        elif name == "zc":
-            z_wait(args[0], 4)
-            go(a_give(args[0]))
+            give(*args)
         elif name == "pk":
             pack(*args)
         elif name == "wo":
@@ -236,45 +274,52 @@
                 back = owner(g, h)
                 origin = lax.rem(y - back + NY, NY)
                 o_copy(r, g, h, origin, dev(dy=back)).wait_recv()
+    for r in range(len(chunks)):
+        for e in (0, 1, 2):
+            share(r, e, 0).wait_send()
+        pl.when(mine)(share(r, 3, 0).wait_send)
     for copy in started:
         copy.wait_send()
 
 
 STEPS = [
-    ("zo", 0), ("wo", 0), ("zo", 1), ("wg",), ("wo", 1), ("zf", 0, 1), ("zo", 2), ("zf", 0, 2), ("zf", 1, 1),
-    ("wf", 0), ("zf", 0, 3), ("zo", 3), ("ws", 0), ("zc", 0), ("zf", 1, 2), ("ws", 1), ("pk", 0), ("mm", 0, 0), ("zf", 2, 1),
-    ("mm", 0, 1), ("zf", 1, 3), ("ra", 0, 0), ("wf", 1), ("ra", 0, 1), ("fi", 0, 0), ("zf", 2, 2), ("fi", 0, 1),
-    ("zc", 1), ("ws", 2), ("mm", 0, 2), ("zf", 3, 1), ("pk", 1), ("mm", 1, 0), ("ra", 0, 2), ("zf", 2, 3), ("mm", 1, 1),
-    ("ra", 1, 0), ("fi", 0, 2), ("mm", 1, 2), ("zf", 3, 2), ("ra", 1, 1), ("zc", 2), ("fi", 1, 0), ("ra", 1, 2), ("wf", 2), ("fi", 1, 1),
-    ("pk", 2), ("mm", 2, 0), ("fi", 1, 2), ("zf", 3, 3), ("mm", 2, 1), ("ws", 3), ("ra", 2, 0), ("mm", 2, 2), ("ra", 2, 1), ("fi", 2, 0),
-    ("mm", 0, 3), ("ra", 2, 2), ("zc", 3), ("fi", 2, 1), ("mm", 1, 3), ("ra", 0, 3), ("fi", 2, 2), ("mm", 2, 3), ("ra", 1, 3), ("fi", 0, 3),
-    ("pk", 3), ("mm", 3, 0), ("ra", 2, 3), ("fi", 1, 3), ("mm", 3, 1), ("ra", 3, 0), ("fi", 2, 3), ("mm", 3, 2), ("ra", 3, 1), ("fi", 3, 0),
-    ("mm", 3, 3), ("ra", 3, 2), ("fi", 3, 1), ("ra", 3, 3), ("fi", 3, 2), ("fi", 3, 3),
+    ("wo", 0), ("zo", 0), ("wg",), ("zo", 1), ("wo", 1), ("zo", 2), ("ws", 0), ("zf", 0, 1), ("zf", 1, 1), ("zo", 3),
+    ("wf", 0), ("zf", 0, 2), ("zf", 1, 2), ("ws", 1), ("zf", 0, 3), ("zf", 2, 1), ("wf", 1), ("zf", 1, 3),
+    ("zf", 3, 1), ("pk", 0), ("ws", 2), ("mm", 0, 1), ("mm", 0, 2), ("zf", 2, 2), ("mm", 0, 0), ("pk", 1),
+    ("mm", 1, 1), ("mm", 1, 2), ("zf", 3, 2), ("mm", 1, 0), ("wf", 2), ("ra", 0, 1), ("zf", 2, 3), ("ra", 0, 2),
+    ("ra", 0, 0), ("ra", 1, 1), ("ws", 3), ("mm", 0, 3), ("zf", 3, 3), ("ra", 1, 2), ("mm", 1, 3), ("ra", 1, 0),
+    ("pk", 2), ("fi", 0, 1), ("mm", 2, 1), ("fi", 0, 2), ("fi", 0, 0), ("mm", 2, 2), ("fi", 1, 1), ("ra", 0, 3),
+    ("pk", 3), ("mm", 2, 3), ("fi", 1, 2), ("ra", 1, 3), ("mm", 3, 1), ("fi", 1, 0), ("mm", 3, 2), ("ra", 2, 1),
+    ("mm", 3, 3), ("ra", 2, 2), ("fi", 0, 3), ("ra", 2, 3), ("mm", 2, 0), ("fi", 1, 3), ("ra", 3, 1), ("mm", 3, 0),
+    ("ra", 3, 2), ("fi", 2, 1), ("ra", 3, 3), ("fi", 2, 2), ("fi", 2, 3), ("ra", 2, 0), ("fi", 3, 1), ("ra", 3, 0),
+    ("fi", 3, 2), ("fi", 3, 3), ("fi", 2, 0), ("fi", 3, 0),
 ]
 
 
 def on_device(amplitudes, integrals, row_irreps, col_irreps):
     count, bf16, dma = len(CHUNKS), jnp.bfloat16, pltpu.SemaphoreType.DMA
-    any_space, smem, vmem = (pl.BlockSpec(memory_space=s) for s in (pl.ANY, pltpu.SMEM, pltpu.VMEM))
+    hbm, vmem = (pl.BlockSpec(memory_space=s) for s in (pltpu.HBM, pltpu.VMEM))
     return pl.pallas_call(
         functools.partial(kernel, STEPS),
         out_shape=jax.ShapeDtypeStruct((1024, 256), bf16),
-        in_specs=[any_space, any_space, smem, smem],
+        in_specs=[hbm] * 4,
         out_specs=vmem,
         scratch_shapes=[
+            pltpu.SMEM((1, 2), jnp.int32),
+            pltpu.SMEM((2, 2), jnp.int32),
             pltpu.VMEM((8, 256, 512), bf16),
             pltpu.VMEM((4, 256, 512), bf16),
             pltpu.VMEM((2, 512, 1024), bf16),
             pltpu.VMEM((4, 2, 256, 1024), bf16),
             pltpu.VMEM((4, 1024, 256), jnp.float32),
-            pltpu.VMEM((1024, 256), bf16),
-            pltpu.VMEM((1024, 256), bf16),
             pltpu.VMEM((2, 1024, 256), bf16),
             pltpu.VMEM((2, 1024, 256), bf16),
+            pltpu.VMEM((2, 512, 256), bf16),
+            pltpu.VMEM((2, 512, 256), bf16),
             pltpu.VMEM((1024, 256), bf16),
-            dma((2,)),
-            dma((count, 2, 4)), dma((count, 2, 4)),
-            dma((count,)), dma((count,)),
+            dma((4,)),
+            dma((count, 2, 4)), dma((count, 2, 4)), dma((count, 2)),
+            dma((count, 4)), dma((count, 4)),
             dma((2, 3)), dma((2, 3)),
             dma((4,)), dma((4,)),
             dma((4 * count, 2)), dma((4 * count, 2)),
@@ -282,7 +327,7 @@
             dma((4 * count, 2)), dma((4 * count, 2)),
         ],
         compiler_params=pltpu.CompilerParams(
-            collective_id=0, has_side_effects=True, vmem_limit_bytes=48 * 2**20
+            collective_id=0, has_side_effects=True, vmem_limit_bytes=56 * 2**20
         ),
         cost_estimate=pl.CostEstimate(flops=2 * 2**30, bytes_accessed=2 * 2**20, transcendentals=0),
         name="ladder",

time: 84.3 us -> 54.5 us (0.65)
  the two profiles are of different devices: /device:TPU:32 before, /device:TPU:2 now
where the time goes in v2:
time: 54.5 us; the launch traced here: 54.4 us
  Pallas kernels  52.5 us (96%)
  local copies, waits for them, and re-layouts  1.87 us (3%)
    pallas_call x1, Pallas kernels, on_device(): pl.pallas_call(functools.partial(kernel, STEPS), out_shape=jax.ShapeDtype...  52.5 us
    unnamed x1, local copies, waits for them, and re-layouts  1.87 us

profile of v2, /device:TPU:2, one launch (start us, length us, event | category | flops | bytes accessed | tf_op | source)
XLA Modules:
  0.0 54.4 jit_solution(6901185277381426254)
XLA Ops:
  0.0 52.5 %ladder.1 = bf16[1024,256]{1,0:T(8,128)(2,1)} custom-call(bf16[256,512]{1,0:T(8,128)(2,1)} %amp.1, bf16[2,256,512]{2,1,0:T(8,128)(2,1)} %integ.1, s32[1,2]{1,0:T(1,128)} %row_hbm.1, s32[2,2]{1,0:T(2,128)} %col_hbm.1), custom_call_target="tpu_custom_call" | custom-call | flops 2147483648 | bytes 2097152 | tf_op jit(solution)/shard_map/ladder/pallas_call | solution.py:302
  52.5 1.9 %copy.6 = bf16[1024,256]{1,0:T(8,128)(2,1)} copy(bf16[1024,256]{1,0:T(8,128)(2,1)} %ladder.1) | data formatting | bytes 1048576

commit v3 on v2

--- a/solution.py
+++ b/solution.py
@@ -23,7 +23,7 @@
 def kernel(
     steps, amp, integ, row_hbm, col_hbm, out, row_ir, col_ir,
     ag, asib, pk, wb, cp, sx1, rx1, sx2, rx2, res,
-    loc, zs, zr, zq, ds, dr, ys, yr, ws, wr, x1s, x1r, x2s, x2r, os, orr,
+    loc, sent, zr, pr, yr, wr, x1r, x2r, orr,
 ):
     x, y, z, c = coordinates()
     sib = 1 - c
@@ -57,16 +57,16 @@
     ]
     for partner in partners:
         pl.semaphore_signal(barrier, inc=1, device_id=partner, device_id_type=MESH)
-    started = []
-
     def remote(src, dst, send, recv, to):
         return pltpu.make_async_remote_copy(
             src_ref=src, dst_ref=dst, send_sem=send, recv_sem=recv, device_id=to, device_id_type=MESH
         )
 
-    def go(copy):
-        copy.start()
-        started.append(copy)
+    def arrived(ref, recv):
+        remote(ref, ref, sent.at[0], recv, dev(flip=True)).wait_recv()
+
+    def left(ref, send):
+        remote(ref, ref, sent.at[send], orr, dev(flip=True)).wait_send()
 
     mine = lax.rem(z, 2) == c
 
@@ -79,42 +79,40 @@
     def z_copy(r, s, d, behind):
         sign = 1 if s == 0 else -1
         block = ag.at[lax.rem(z - sign * behind + NZ, NZ), z_rows(r, s, d)]
-        return remote(block, block, zs.at[r, s, d - 1], zr.at[r, s, d - 1], dev(dz=sign))
+        return remote(block, block, sent.at[0], zr.at[r, d - 1] if d < 4 else pr.at[r], dev(dz=sign))
 
     def cross_copy(r, s, behind):
         sign = 1 if s == 0 else -1
         origin = lax.rem(z - sign * behind + NZ, NZ)
         rows = z_rows(r, s, 4)
         return remote(
-            ag.at[origin, rows], asib.at[lax.div(origin, 2), rows], zs.at[r, s, 3], zq.at[r, s], dev(dz=sign, flip=True)
+            ag.at[origin, rows], asib.at[lax.div(origin, 2), rows], sent.at[0], pr.at[r], dev(dz=sign, flip=True)
         )
 
     def z_send(r, d):
         for s in (0, 1):
             copy = z_copy(r, s, d, d - 1)
             if d < 4:
-                go(copy)
+                copy.start()
             else:
                 pl.when(jnp.logical_not(mine))(copy.start)
                 pl.when(mine)(cross_copy(r, s, 3).start)
-                started.append(copy)
 
     def z_wait(r, d):
-        for s in (0, 1):
-            z_copy(r, s, d, d).wait_recv()
-
-    def share(r, e, far):
+        arrived(ag.at[pl.ds(0, 2), z_rows(r, 0, d)], zr.at[r, d - 1])
+
+    def share(r, far):
         origin = lax.rem(z + far + NZ, NZ)
         rows = pl.ds(starts[r], chunks[r])
         return remote(
-            ag.at[origin, rows], asib.at[lax.div(origin, 2), rows], ds.at[r, e], dr.at[r, e], dev(flip=True)
+            ag.at[origin, rows], asib.at[lax.div(origin, 2), rows], sent.at[1], pr.at[r], dev(flip=True)
         )
 
     def give(r, d):
-        sends = {0: ((2, 0),), 1: ((0, 1), (1, -1)), 2: ((0, 2), (1, -2)), 3: ((2, 3), (3, -3))}[d]
+        sends = {0: (0,), 1: (1, -1), 2: (2, -2), 3: (3, -3)}[d]
         def act():
-            for e, far in sends:
-                share(r, e, far).start()
+            for far in sends:
+                share(r, far).start()
         pl.when(mine if d % 2 else jnp.logical_not(mine))(act)
 
     def y_half(s, n):
@@ -125,25 +123,25 @@
         half = pl.ds(128 * y_half(s, n), 128)
         src = wb.at[0 if n < 2 else 1, :, half, pl.ds(0, 512)]
         dst = wb.at[n + 1, :, half, pl.ds(0, 512)]
-        return remote(src, dst, ys.at[s, n], yr.at[s, n], dev(dy=sign))
+        return remote(src, dst, sent.at[2], yr.at[n], dev(dy=sign))
 
     def w_give(g):
         return remote(
-            wb.at[g, :, :, pl.ds(0, 512)], wb.at[g, :, :, pl.ds(512, 512)], ws.at[g], wr.at[g], dev(flip=True)
+            wb.at[g, :, :, pl.ds(0, 512)], wb.at[g, :, :, pl.ds(512, 512)], sent.at[3], wr.at[g], dev(flip=True)
         )
 
     def x1_copy(r, g, s):
         t, off = tiles[r, g]
         rows = pl.ds(off, chunks[r])
         return remote(
-            sx1.at[s, rows], rx1.at[s, rows], x1s.at[t, s], x1r.at[t, s], dev(dx=1 if s == 0 else -1)
+            sx1.at[s, rows], rx1.at[s, rows], sent.at[4], x1r.at[t], dev(dx=1 if s == 0 else -1)
         )
 
     def x2_copy(r, g, s):
         t, off = tiles[r, g]
         rows = pl.ds(off // 2, chunks[r] // 2)
         return remote(
-            sx2.at[s, rows], rx2.at[s, rows], x2s.at[t, s], x2r.at[t, s], dev(dx=1 if s == 0 else -1)
+            sx2.at[s, rows], rx2.at[s, rows], sent.at[5], x2r.at[t], dev(dx=1 if s == 0 else -1)
         )
 
     def owner(g, h):
@@ -153,7 +151,7 @@
         t, off = tiles[r, g]
         cols = pl.ds(128 * h, 128)
         dst = out.at[pl.ds(pl.multiple_of(origin * 256 + starts[r], 32), chunks[r]), cols]
-        return remote(res.at[pl.ds(off, chunks[r]), cols], dst, os.at[t, h], orr.at[t, h], to)
+        return remote(res.at[pl.ds(off, chunks[r]), cols], dst, sent.at[6], orr, to)
 
     def multiply(r, g):
         t, off = tiles[r, g]
@@ -173,24 +171,23 @@
             target = lax.rem(x + (1 if s == 0 else 3), NX)
             sx1[s, pl.ds(off, half)] = cp[lax.rem(x + 2, NX), pl.ds(off + s * half, half)].astype(jnp.bfloat16)
             sx1[s, pl.ds(off + half, half)] = cp[target, pl.ds(off + (1 - s) * half, half)].astype(jnp.bfloat16)
-            go(x1_copy(r, g, s))
+            x1_copy(r, g, s).start()
 
     def add_on(r, g):
         t, off = tiles[r, g]
         half = chunks[r] // 2
-        for s in (0, 1):
-            x1_copy(r, g, s).wait_recv()
+        arrived(rx1.at[:, pl.ds(off, chunks[r])], x1r.at[t])
+        for s in (0, 1):
             target = lax.rem(x + (1 if s == 0 else 3), NX)
             value = cp[target, pl.ds(off + s * half, half)] + rx1[s, pl.ds(off, half)].astype(jnp.float32)
             sx2[s, pl.ds(off // 2, half)] = value.astype(jnp.bfloat16)
-            go(x2_copy(r, g, s))
+            x2_copy(r, g, s).start()
 
     def finish(r, g):
         t, off = tiles[r, g]
         n = chunks[r]
         half = n // 2
-        for s in (0, 1):
-            x2_copy(r, g, s).wait_recv()
+        arrived(rx2.at[:, pl.ds(off // 2, half)], x2r.at[t])
         for s in (0, 1):
             total = (
                 cp[x, pl.ds(off + s * half, half)]
@@ -203,19 +200,13 @@
                 res[pl.ds(off + s * half, half)] = total
         if g > 0:
             for h in (0, 1):
-                go(o_copy(r, g, h, y, dev(dy=owner(g, h))))
+                o_copy(r, g, h, y, dev(dy=owner(g, h))).start()
 
     def pack(r):
-        for e in (0, 1, 2):
-            share(r, e, 0).wait_recv()
-        pl.when(jnp.logical_not(mine))(share(r, 3, 0).wait_recv)
-        def last_hop():
-            for s in (0, 1):
-                z_copy(r, s, 4, 4).wait_recv()
-                cross_copy(r, s, 4).wait_recv()
-        pl.when(mine)(last_hop)
+        rows = pl.ds(starts[r], chunks[r])
+        pl.when(mine)(lambda: arrived(ag.at[pl.ds(0, 5), rows], pr.at[r]))
+        pl.when(jnp.logical_not(mine))(lambda: arrived(ag.at[pl.ds(0, 4), rows], pr.at[r]))
         n = chunks[r]
-        rows = pl.ds(starts[r], n)
         for i in (0, 1):
             to = pl.ds(2 * starts[r] + i * n, n)
             for k, (direct, mirror) in enumerate((
@@ -250,16 +241,15 @@
             pack(*args)
         elif name == "wo":
             for s in (0, 1):
-                go(y_copy(s, args[0]))
+                y_copy(s, args[0]).start()
         elif name == "wg":
-            go(w_give(0))
+            w_give(0).start()
         elif name == "wf":
-            for s in (0, 1):
-                y_copy(s, args[0]).wait_recv()
+            arrived(wb.at[args[0] + 1, :, :, pl.ds(0, 512)], yr.at[args[0]])
             if args[0] == 0:
                 for s in (0, 1):
-                    go(y_copy(s, 2))
-            go(w_give(args[0] + 1))
+                    y_copy(s, 2).start()
+            w_give(args[0] + 1).start()
         elif name == "ws":
             w_give(args[0]).wait_recv()
         elif name == "mm":
@@ -268,18 +258,15 @@
             add_on(*args)
         elif name == "fi":
             finish(*args)
-    for r in range(len(chunks)):
-        for g in (1, 2, 3):
-            for h in (0, 1):
-                back = owner(g, h)
-                origin = lax.rem(y - back + NY, NY)
-                o_copy(r, g, h, origin, dev(dy=back)).wait_recv()
-    for r in range(len(chunks)):
-        for e in (0, 1, 2):
-            share(r, e, 0).wait_send()
-        pl.when(mine)(share(r, 3, 0).wait_send)
-    for copy in started:
-        copy.wait_send()
+    arrived(out.at[pl.ds(0, 768)], orr)
+    left(ag.at[pl.ds(0, 7)], 0)
+    pl.when(mine)(lambda: left(ag.at[pl.ds(0, 4)], 1))
+    pl.when(jnp.logical_not(mine))(lambda: left(ag.at[pl.ds(0, 3)], 1))
+    left(wb.at[pl.ds(0, 3), :, :, pl.ds(0, 512)], 2)
+    left(wb.at[:, :, :, pl.ds(0, 512)], 3)
+    left(sx1, 4)
+    left(sx2, 5)
+    left(res.at[pl.ds(0, 768)], 6)
 
 
 STEPS = [
@@ -318,20 +305,14 @@
             pltpu.VMEM((2, 512, 256), bf16),
             pltpu.VMEM((1024, 256), bf16),
             dma((4,)),
-            dma((count, 2, 4)), dma((count, 2, 4)), dma((count, 2)),
-            dma((count, 4)), dma((count, 4)),
-            dma((2, 3)), dma((2, 3)),
-            dma((4,)), dma((4,)),
-            dma((4 * count, 2)), dma((4 * count, 2)),
-            dma((4 * count, 2)), dma((4 * count, 2)),
-            dma((4 * count, 2)), dma((4 * count, 2)),
+            dma((7,)), dma((count, 3)), dma((count,)), dma((3,)), dma((4,)), dma((4 * count,)), dma((4 * count,)), dma,
         ],
         compiler_params=pltpu.CompilerParams(
-            collective_id=0, has_side_effects=True, vmem_limit_bytes=56 * 2**20
+            collective_id=0, has_side_effects=True, vmem_limit_bytes=48 * 2**20
         ),
         cost_estimate=pl.CostEstimate(flops=2 * 2**30, bytes_accessed=2 * 2**20, transcendentals=0),
         name="ladder",
-    )(amplitudes, integrals, row_irreps, col_irreps)
+    )(*(pltpu.with_memory_space_constraint(a, pltpu.HBM) for a in (amplitudes, integrals, row_irreps, col_irreps)))
 
 
 def solution(mesh):

time: 54.5 us -> 50.1 us (0.919)
  the two profiles are of different devices: /device:TPU:2 before, /device:TPU:32 now
where the time goes in v3:
time: 50.1 us; the launch traced here: 49.1 us
  Pallas kernels  48.3 us (96%)
  local copies, waits for them, and re-layouts  0.8 us (2%)
    pallas_call x1, Pallas kernels, on_device(): pl.pallas_call(functools.partial(kernel, STEPS), out_shape=jax.ShapeDtype...  48.3 us

profile of v3, /device:TPU:32, one launch (start us, length us, event | category | flops | bytes accessed | tf_op | source)
XLA Modules:
  0.0 49.1 jit_solution(7287996399559108586)
XLA Ops:
  0.0 48.3 %ladder.1 = bf16[1024,256]{1,0:T(8,128)(2,1)S(1)} custom-call(bf16[256,512]{1,0:T(8,128)(2,1)} %amp.1, bf16[2,256,512]{2,1,0:T(8,128)(2,1)} %integ.1, s32[1,2]{1,0:T(1,128)} %row_hbm.1, s32[2,2]{1,0:T(2,128)} %col_hbm.1), custom_call_target="tpu_custom_call" | custom-call | flops 2147483648 | bytes 2097152 | tf_op jit(solution)/shard_map/ladder/pallas_call | solution.py:289
  48.4 0.8 %copy.6 = bf16[1024,256]{1,0:T(8,128)(2,1)} copy(bf16[1024,256]{1,0:T(8,128)(2,1)S(1)} %ladder.1) | data formatting | bytes 1048576

commit v4 on v3

v4 whole, which is shorter than its diff:
```python
import jax
import jax.numpy as jnp
from jax import lax
from jax.experimental import pallas as pl
from jax.experimental.pallas import tpu as pltpu
from jax.sharding import PartitionSpec as P

MESH = pl.DeviceIdType.MESH
NX, NY, NZ = 4, 4, 8

CHUNKS = (64, 64, 64, 64)


def coordinates():
    pair, cd = lax.axis_index("pair"), lax.axis_index("cd")
    return lax.div(cd, 2), lax.rem(pair, NY), lax.div(pair, NY), lax.rem(cd, 2)


def kernel(
    amp, integ, row_hbm, col_hbm, out, row_ir, col_ir,
    ag, asib, pk, wb, cp, sx1, rx1, sx2, rx2, res,
    loc, sent, zr, pa, pb, yr, wr, x1r, x2r, orr,
):
    x, y, z, c = coordinates()
    sib = 1 - c
    chunks = CHUNKS
    starts = [sum(chunks[:k]) for k in range(len(chunks))]
    def dev(dx=0, dy=0, dz=0, flip=False):
        return (
            lax.rem(z + dz + NZ, NZ) * NY + lax.rem(y + dy + NY, NY),
            lax.rem(x + dx + NX, NX) * 2 + (sib if flip else c),
        )

    load_a = pltpu.make_async_copy(amp, ag.at[z], loc.at[0])
    load_w = pltpu.make_async_copy(integ, wb.at[0, :, :, pl.ds(0, 512)], loc.at[1])
    loads = [
        load_w,
        pltpu.make_async_copy(row_hbm, row_ir, loc.at[2]),
        pltpu.make_async_copy(col_hbm, col_ir, loc.at[3]),
    ]
    load_a.start()
    for load in loads:
        load.start()
    barrier = pltpu.get_barrier_semaphore()
    partners = [
        dev(dx=1), dev(dx=-1), dev(dy=1), dev(dy=-1), dev(dy=2), dev(dz=1), dev(dz=-1), dev(flip=True),
    ]
    for partner in partners:
        pl.semaphore_signal(barrier, inc=1, device_id=partner, device_id_type=MESH)
    def remote(src, dst, send, recv, to):
        return pltpu.make_async_remote_copy(
            src_ref=src, dst_ref=dst, send_sem=send, recv_sem=recv, device_id=to, device_id_type=MESH
        )

    def arrived(ref, recv):
        remote(ref, ref, sent.at[0], recv, dev(flip=True)).wait_recv()

    def left(ref, send):
        remote(ref, ref, sent.at[send], orr, dev(flip=True)).wait_send()

    mine = lax.rem(z, 2) == c
    first = jnp.where(mine, 1 - lax.div(lax.rem(z, 4), 2), lax.div(lax.rem(z, 4), 2))

    def pair_of(e):
        return first if e == 0 else 1 - first

    def is_target(e):
        return lax.rem(x, 2) == pair_of(e)

    def z_rows(r, s, d):
        if d < 4:
            return pl.ds(starts[r], chunks[r])
        half = chunks[r] // 2
        return pl.ds(starts[r] + (0 if s == 0 else half), half)

    def z_copy(r, s, d, behind):
        sign = 1 if s == 0 else -1
        block = ag.at[lax.rem(z - sign * behind + NZ, NZ), z_rows(r, s, d)]
        return remote(block, block, sent.at[0], zr.at[r, d - 1] if d < 4 else pb.at[r], dev(dz=sign))

    def cross_copy(r, s, behind):
        sign = 1 if s == 0 else -1
        origin = lax.rem(z - sign * behind + NZ, NZ)
        rows = z_rows(r, s, 4)
        return remote(
            ag.at[origin, rows], asib.at[lax.div(origin, 2), rows], sent.at[0], pb.at[r], dev(dz=sign, flip=True)
        )

    def z_send(r, d):
        for s in (0, 1):
            copy = z_copy(r, s, d, d - 1)
            if d < 4:
                copy.start()
            else:
                pl.when(jnp.logical_not(mine))(copy.start)
                pl.when(mine)(cross_copy(r, s, 3).start)

    def z_wait(r, d):
        arrived(ag.at[pl.ds(0, 2), z_rows(r, 0, d)], zr.at[r, d - 1])

    def share(r, far):
        origin = lax.rem(z + far + NZ, NZ)
        rows = pl.ds(starts[r], chunks[r])
        return remote(
            ag.at[origin, rows], asib.at[lax.div(origin, 2), rows], sent.at[1], (pa if far else pb).at[r], dev(flip=True)
        )

    def give(r, d):
        sends = {0: (0,), 1: (1, -1), 2: (2, -2), 3: (3, -3)}[d]
        def act():
            for far in sends:
                share(r, far).start()
        pl.when(mine if d % 2 else jnp.logical_not(mine))(act)

    def y_half(s, n):
        return s if n != 1 else 1 - s

    def y_copy(s, n):
        sign = 1 if s == 0 else -1
        half = pl.ds(128 * y_half(s, n), 128)
        src = wb.at[0 if n < 2 else 1, :, half, pl.ds(0, 512)]
        dst = wb.at[n + 1, :, half, pl.ds(0, 512)]
        return remote(src, dst, sent.at[2], yr.at[n], dev(dy=sign))

    def w_give(g):
        return remote(
            wb.at[g, :, :, pl.ds(0, 512)], wb.at[g, :, :, pl.ds(512, 512)], sent.at[3], wr.at[g], dev(flip=True)
        )

    def x1_copy(t, s):
        rows = pl.ds(64 * t, 64)
        return remote(sx1.at[s, rows], rx1.at[s, rows], sent.at[4], x1r.at[t], dev(dx=1 if s == 0 else -1))

    def x2_copy(t, s):
        rows = pl.ds(64 * t, 64)
        return remote(sx2.at[s, rows], rx2.at[s, rows], sent.at[5], x2r.at[t], dev(dx=1 if s == 0 else -1))

    def owner(g, h):
        return {1: (-1, 1), 2: (1, -1), 3: (2, 2)}[g][h]

    def o_copy(b, g, h, to):
        cols = pl.ds(128 * h, 128)
        dst = out.at[pl.ds(pl.multiple_of(y * 256 + 128 * b, 128), 128), cols]
        return remote(res.at[pl.ds(128 * (4 * b + g), 128), cols], dst, sent.at[6], orr, to)

    def tile(b, e, g):
        return (2 * b + e) * 4 + g

    def block_of(dx):
        return lax.div(lax.rem(x + dx + NX, NX), 2)

    def pack(b, e):
        i = pair_of(e)
        for r in (2 * b, 2 * b + 1):
            rows = pl.ds(starts[r], chunks[r])
            if e == 0:
                pl.when(mine)(lambda: arrived(ag.at[pl.ds(0, 2), rows], pa.at[r]))
                pl.when(jnp.logical_not(mine))(lambda: arrived(ag.at[pl.ds(0, 4), rows], pa.at[r]))
            else:
                pl.when(mine)(lambda: arrived(ag.at[pl.ds(0, 3), rows], pb.at[r]))
        rows = pl.ds(128 * b, 128)
        to = pl.ds(128 * (2 * b + e), 128)
        for k, (direct, mirror) in enumerate((
            (ag[c + 2 * i, rows], ag[c + 2 * i + 4, rows]),
            (asib[i, rows], asib[i + 2, rows]),
        )):
            direct, mirror = direct.astype(jnp.float32), mirror.astype(jnp.float32)
            cols = pl.ds(512 * k, 512)
            pk[0, to, cols] = (direct + mirror).astype(jnp.bfloat16)
            pk[1, to, cols] = (direct - mirror).astype(jnp.bfloat16)

    def multiply(b, e, g):
        t = tile(b, e, g)
        rows = pl.ds(128 * (2 * b + e), 128)
        dims = (((1,), (1,)), ((), ()))
        plus = lax.dot_general(pk[0, rows], wb[g, 0], dims, preferred_element_type=jnp.float32)
        minus = lax.dot_general(pk[1, rows], wb[g, 1], dims, preferred_element_type=jnp.float32)
        cp[0, pl.ds(128 * t, 128)] = plus + minus
        cp[1, pl.ds(128 * t, 128)] = plus - minus
        target = is_target(e)
        for s in (0, 1):
            block = jnp.where(target, block_of(2), block_of(1 if s == 0 else -1))
            half = jnp.where(target, s, 1 - s)
            part = pl.ds(pl.multiple_of(128 * t + 64 * half, 64), 64)
            sx1[s, pl.ds(64 * t, 64)] = cp[block, part].astype(jnp.bfloat16)
            x1_copy(t, s).start()

    def add_on(b, e, g):
        t = tile(b, e, g)
        rows = pl.ds(64 * t, 64)
        def act():
            arrived(rx1.at[:, rows], x1r.at[t])
            for s in (0, 1):
                value = cp[block_of(1 if s == 0 else -1), pl.ds(128 * t + 64 * s, 64)]
                sx2[s, rows] = (value + rx1[s, rows].astype(jnp.float32)).astype(jnp.bfloat16)
                x2_copy(t, s).start()
        pl.when(jnp.logical_not(is_target(e)))(act)

    def finish(b, e, g):
        t = tile(b, e, g)
        rows = pl.ds(64 * t, 64)
        def act():
            arrived(rx1.at[:, rows], x1r.at[t])
            arrived(rx2.at[:, rows], x2r.at[t])
            for s in (0, 1):
                total = (
                    cp[block_of(0), pl.ds(128 * t + 64 * s, 64)]
                    + rx2[s, rows].astype(jnp.float32)
                    + rx1[1 - s, rows].astype(jnp.float32)
                ).astype(jnp.bfloat16)
                if g == 0:
                    out[pl.ds(pl.multiple_of(y * 256 + 128 * b + 64 * s, 64), 64)] = total
                else:
                    res[pl.ds(128 * (4 * b + g) + 64 * s, 64)] = total
            if g > 0:
                for h in (0, 1):
                    o_copy(b, g, h, dev(dy=owner(g, h))).start()
        pl.when(is_target(e))(act)

    def mask_own():
        for load in loads:
            load.wait()
        row_sym = row_ir[0, 0] ^ row_ir[0, 1]
        for k in (0, 1):
            keep = (row_sym == (col_ir[k, 0] ^ col_ir[k, 1])).astype(jnp.int32).astype(jnp.float32)
            cols = pl.ds(256 * k, 256)
            for s in (0, 1):
                wb[0, s, :, cols] = (wb[0, s, :, cols].astype(jnp.float32) * keep).astype(jnp.bfloat16)

    load_a.wait()
    pl.semaphore_wait(barrier, len(partners))

    def perform(steps):
        for step in steps:
            name, args = step[0], step[1:]
            if name == "zo":
                z_send(args[0], 1)
                give(args[0], 0)
            elif name == "zf":
                z_wait(*args)
                z_send(args[0], args[1] + 1)
                give(*args)
            elif name == "pk":
                pack(*args)
            elif name == "wo":
                for s in (0, 1):
                    y_copy(s, args[0]).start()
            elif name == "wk":
                mask_own()
            elif name == "wg":
                w_give(0).start()
            elif name == "wf":
                arrived(wb.at[args[0] + 1, :, :, pl.ds(0, 512)], yr.at[args[0]])
                if args[0] == 0:
                    for s in (0, 1):
                        y_copy(s, 2).start()
                w_give(args[0] + 1).start()
            elif name == "ws":
                w_give(args[0]).wait_recv()
            elif name == "mm":
                multiply(*args)
            elif name == "ra":
                add_on(*args)
            elif name == "fi":
                finish(*args)

    pl.when(mine)(lambda: perform(STEPS_MINE))
    pl.when(jnp.logical_not(mine))(lambda: perform(STEPS_OTHER))
    arrived(out.at[pl.ds(0, 768)], orr)
    left(ag.at[pl.ds(0, 7)], 0)
    pl.when(mine)(lambda: left(ag.at[pl.ds(0, 4)], 1))
    pl.when(jnp.logical_not(mine))(lambda: left(ag.at[pl.ds(0, 3)], 1))
    left(wb.at[pl.ds(0, 3), :, :, pl.ds(0, 512)], 2)
    left(wb.at[:, :, :, pl.ds(0, 512)], 3)
    left(sx1, 4)
    left(sx2.at[:, pl.ds(0, 512)], 5)
    left(res.at[pl.ds(0, 768)], 6)


STEPS_MINE = [
    ("zo", 0), ("zo", 1), ("wk",), ("wo", 0), ("zo", 2), ("wo", 1), ("zf", 0, 1), ("zf", 1, 1), ("zo", 3), ("wg",),
    ("wf", 0), ("zf", 0, 2), ("zf", 1, 2), ("zf", 2, 1), ("ws", 0), ("ws", 1), ("pk", 0, 0), ("mm", 0, 0, 1),
    ("mm", 0, 0, 0), ("zf", 0, 3), ("zf", 3, 1), ("zf", 1, 3), ("wf", 1), ("ra", 0, 0, 1), ("ra", 0, 0, 0),
    ("zf", 2, 2), ("ws", 2), ("mm", 0, 0, 2), ("zf", 3, 2), ("fi", 0, 0, 1), ("fi", 0, 0, 0), ("pk", 0, 1),
    ("mm", 0, 1, 1), ("mm", 0, 1, 2), ("wf", 2), ("zf", 2, 3), ("ra", 0, 0, 2), ("pk", 1, 0), ("mm", 1, 0, 1),
    ("mm", 1, 0, 2), ("zf", 3, 3), ("ws", 3), ("mm", 0, 0, 3), ("mm", 0, 1, 3), ("mm", 1, 0, 3), ("ra", 0, 1, 1),
    ("ra", 0, 1, 2), ("ra", 1, 0, 1), ("ra", 1, 0, 2), ("pk", 1, 1), ("mm", 1, 1, 3), ("mm", 1, 1, 1),
    ("mm", 1, 1, 2), ("fi", 0, 0, 2), ("fi", 0, 1, 1), ("fi", 0, 1, 2), ("ra", 0, 0, 3), ("ra", 0, 1, 3),
    ("ra", 1, 0, 3), ("mm", 0, 1, 0), ("ra", 1, 1, 3), ("ra", 1, 1, 1), ("ra", 1, 1, 2), ("fi", 1, 0, 1),
    ("fi", 1, 0, 2), ("mm", 1, 0, 0), ("mm", 1, 1, 0), ("fi", 0, 0, 3), ("fi", 0, 1, 3), ("fi", 1, 0, 3),
    ("fi", 1, 1, 3), ("fi", 1, 1, 1), ("fi", 1, 1, 2), ("ra", 0, 1, 0), ("ra", 1, 0, 0), ("ra", 1, 1, 0),
    ("fi", 0, 1, 0), ("fi", 1, 0, 0), ("fi", 1, 1, 0),
]

STEPS_OTHER = [
    ("zo", 0), ("zo", 1), ("wk",), ("wo", 0), ("zo", 2), ("wo", 1), ("zf", 0, 1), ("zf", 1, 1), ("zo", 3), ("wg",),
    ("wf", 0), ("zf", 0, 2), ("zf", 1, 2), ("zf", 2, 1), ("ws", 0), ("ws", 1), ("zf", 0, 3), ("zf", 3, 1),
    ("zf", 1, 3), ("wf", 1), ("zf", 2, 2), ("pk", 0, 0), ("mm", 0, 0, 1), ("mm", 0, 0, 0), ("pk", 0, 1),
    ("mm", 0, 1, 1), ("zf", 3, 2), ("mm", 0, 1, 0), ("ws", 2), ("mm", 0, 0, 2), ("mm", 0, 1, 2), ("ra", 0, 0, 1),
    ("wf", 2), ("zf", 2, 3), ("ra", 0, 0, 0), ("ra", 0, 1, 1), ("ra", 0, 1, 0), ("zf", 3, 3), ("ra", 0, 0, 2),
    ("ra", 0, 1, 2), ("ws", 3), ("mm", 0, 0, 3), ("mm", 0, 1, 3), ("pk", 1, 0), ("pk", 1, 1), ("mm", 1, 0, 3),
    ("mm", 1, 1, 3), ("fi", 0, 0, 1), ("fi", 0, 1, 1), ("mm", 1, 0, 1), ("mm", 1, 1, 1), ("ra", 0, 0, 3),
    ("ra", 0, 1, 3), ("fi", 0, 0, 2), ("fi", 0, 1, 2), ("mm", 1, 0, 2), ("mm", 1, 1, 2), ("ra", 1, 0, 3),
    ("ra", 1, 1, 3), ("fi", 0, 0, 0), ("fi", 0, 1, 0), ("fi", 0, 0, 3), ("fi", 0, 1, 3), ("ra", 1, 0, 1),
    ("ra", 1, 1, 1), ("mm", 1, 0, 0), ("mm", 1, 1, 0), ("ra", 1, 0, 2), ("ra", 1, 1, 2), ("fi", 1, 0, 3),
    ("fi", 1, 1, 3), ("fi", 1, 0, 1), ("fi", 1, 1, 1), ("ra", 1, 0, 0), ("ra", 1, 1, 0), ("fi", 1, 0, 2),
    ("fi", 1, 1, 2), ("fi", 1, 0, 0), ("fi", 1, 1, 0),
]


def on_device(amplitudes, integrals, row_irreps, col_irreps):
    count, bf16, dma = len(CHUNKS), jnp.bfloat16, pltpu.SemaphoreType.DMA
    hbm, vmem = (pl.BlockSpec(memory_space=s) for s in (pltpu.HBM, pltpu.VMEM))
    return pl.pallas_call(
        kernel,
        out_shape=jax.ShapeDtypeStruct((1024, 256), bf16),
        in_specs=[hbm] * 4,
        out_specs=vmem,
        scratch_shapes=[
            pltpu.SMEM((1, 2), jnp.int32),
            pltpu.SMEM((2, 2), jnp.int32),
            pltpu.VMEM((8, 256, 512), bf16),
            pltpu.VMEM((4, 256, 512), bf16),
            pltpu.VMEM((2, 512, 1024), bf16),
            pltpu.VMEM((4, 2, 256, 1024), bf16),
            pltpu.VMEM((2, 2048, 256), jnp.float32),
            pltpu.VMEM((2, 1024, 256), bf16),
            pltpu.VMEM((2, 1024, 256), bf16),
            pltpu.VMEM((2, 1024, 256), bf16),
            pltpu.VMEM((2, 1024, 256), bf16),
            pltpu.VMEM((1024, 256), bf16),
            dma((4,)),
            dma((7,)), dma((count, 3)), dma((count,)), dma((count,)), dma((3,)), dma((4,)), dma((16,)), dma((16,)), dma,
        ],
        compiler_params=pltpu.CompilerParams(
            collective_id=0, has_side_effects=True, vmem_limit_bytes=48 * 2**20
        ),
        cost_estimate=pl.CostEstimate(flops=2 * 2**30, bytes_accessed=2 * 2**20, transcendentals=0),
        name="ladder",
    )(*(pltpu.with_memory_space_constraint(a, pltpu.HBM) for a in (amplitudes, integrals, row_irreps, col_irreps)))


def solution(mesh):
    in_specs = (P("pair", "cd"), P(None, "pair", "cd"), P("pair", None), P("cd", None))
    out_specs = P("cd", "pair")
    return jax.shard_map(
        on_device, mesh=mesh, in_specs=in_specs, out_specs=out_specs, check_vma=False
    )
```

time: 50.1 us -> 49.1 us (0.980); the launches traced: 49.1 us -> 49 us
  no operation moved by 1% of the time
where the time goes in v4:
time: 49.1 us; the launch traced here: 49 us
  Pallas kernels  48.2 us (98%)
  local copies, waits for them, and re-layouts  0.8 us (2%)
    pallas_call x1, Pallas kernels, on_device(): pl.pallas_call(kernel, out_shape=jax.ShapeDtypeStruct((1024, 256), bf16),...  48.2 us

profile of v4, /device:TPU:32, one launch (start us, length us, event | category | flops | bytes accessed | tf_op | source)
XLA Modules:
  0.0 49.0 jit_solution(364993671181795740)
XLA Ops:
  0.0 48.2 %ladder.1 = bf16[1024,256]{1,0:T(8,128)(2,1)S(1)} custom-call(bf16[256,512]{1,0:T(8,128)(2,1)} %amp.1, bf16[2,256,512]{2,1,0:T(8,128)(2,1)} %integ.1, s32[1,2]{1,0:T(1,128)} %row_hbm.1, s32[2,2]{1,0:T(2,128)} %col_hbm.1), custom_call_target="tpu_custom_call" | custom-call | flops 2147483648 | bytes 2097152 | tf_op jit(solution)/shard_map/ladder/pallas_call | solution.py:314
  48.2 0.8 %copy.6 = bf16[1024,256]{1,0:T(8,128)(2,1)} copy(bf16[1024,256]{1,0:T(8,128)(2,1)S(1)} %ladder.1) | data formatting | bytes 1048576

commit v5 on v4

--- a/solution.py
+++ b/solution.py
@@ -299,10 +299,10 @@
     ("mm", 0, 1, 1), ("zf", 3, 2), ("mm", 0, 1, 0), ("ws", 2), ("mm", 0, 0, 2), ("mm", 0, 1, 2), ("ra", 0, 0, 1),
     ("wf", 2), ("zf", 2, 3), ("ra", 0, 0, 0), ("ra", 0, 1, 1), ("ra", 0, 1, 0), ("zf", 3, 3), ("ra", 0, 0, 2),
     ("ra", 0, 1, 2), ("ws", 3), ("mm", 0, 0, 3), ("mm", 0, 1, 3), ("pk", 1, 0), ("pk", 1, 1), ("mm", 1, 0, 3),
-    ("mm", 1, 1, 3), ("fi", 0, 0, 1), ("fi", 0, 1, 1), ("mm", 1, 0, 1), ("mm", 1, 1, 1), ("ra", 0, 0, 3),
-    ("ra", 0, 1, 3), ("fi", 0, 0, 2), ("fi", 0, 1, 2), ("mm", 1, 0, 2), ("mm", 1, 1, 2), ("ra", 1, 0, 3),
-    ("ra", 1, 1, 3), ("fi", 0, 0, 0), ("fi", 0, 1, 0), ("fi", 0, 0, 3), ("fi", 0, 1, 3), ("ra", 1, 0, 1),
-    ("ra", 1, 1, 1), ("mm", 1, 0, 0), ("mm", 1, 1, 0), ("ra", 1, 0, 2), ("ra", 1, 1, 2), ("fi", 1, 0, 3),
+    ("mm", 1, 1, 3), ("mm", 1, 0, 1), ("mm", 1, 1, 1), ("mm", 1, 0, 2), ("mm", 1, 1, 2), ("fi", 0, 0, 1),
+    ("fi", 0, 1, 1), ("ra", 0, 0, 3), ("ra", 0, 1, 3), ("fi", 0, 0, 2), ("fi", 0, 1, 2), ("ra", 1, 0, 3),
+    ("ra", 1, 1, 3), ("fi", 0, 0, 0), ("fi", 0, 1, 0), ("ra", 1, 0, 1), ("ra", 1, 1, 1), ("mm", 1, 0, 0),
+    ("mm", 1, 1, 0), ("fi", 0, 0, 3), ("fi", 0, 1, 3), ("ra", 1, 0, 2), ("ra", 1, 1, 2), ("fi", 1, 0, 3),
     ("fi", 1, 1, 3), ("fi", 1, 0, 1), ("fi", 1, 1, 1), ("ra", 1, 0, 0), ("ra", 1, 1, 0), ("fi", 1, 0, 2),
     ("fi", 1, 1, 2), ("fi", 1, 0, 0), ("fi", 1, 1, 0),
 ]

time: 49.1 us -> 48.2 us (0.982)
  Pallas kernels: 48.2 us -> 47.3 us
    pallas_call x1, Pallas kernels: 48.2 us -> 47.3 us  [on_device(): pl.pallas_call(kernel, out_shape=jax.ShapeDtypeStruct((1024, 256), bf16),...]
where the time goes in v5:
time: 48.2 us; the launch traced here: 48.1 us
  Pallas kernels  47.3 us (98%)
  local copies, waits for them, and re-layouts  0.8 us (2%)
    pallas_call x1, Pallas kernels, on_device(): pl.pallas_call(kernel, out_shape=jax.ShapeDtypeStruct((1024, 256), bf16),...  47.3 us

profile of v5, /device:TPU:32, one launch (start us, length us, event | category | flops | bytes accessed | tf_op | source)
XLA Modules:
  0.0 48.1 jit_solution(7359870018330651894)
XLA Ops:
  0.0 47.3 %ladder.1 = bf16[1024,256]{1,0:T(8,128)(2,1)S(1)} custom-call(bf16[256,512]{1,0:T(8,128)(2,1)} %amp.1, bf16[2,256,512]{2,1,0:T(8,128)(2,1)} %integ.1, s32[1,2]{1,0:T(1,128)} %row_hbm.1, s32[2,2]{1,0:T(2,128)} %col_hbm.1), custom_call_target="tpu_custom_call" | custom-call | flops 2147483648 | bytes 2097152 | tf_op jit(solution)/shard_map/ladder/pallas_call | solution.py:314
  47.3 0.8 %copy.6 = bf16[1024,256]{1,0:T(8,128)(2,1)} copy(bf16[1024,256]{1,0:T(8,128)(2,1)S(1)} %ladder.1) | data formatting | bytes 1048576

commit v6 on v5

--- a/solution.py
+++ b/solution.py
@@ -34,11 +34,10 @@
     load_a = pltpu.make_async_copy(amp, ag.at[z], loc.at[0])
     load_w = pltpu.make_async_copy(integ, wb.at[0, :, :, pl.ds(0, 512)], loc.at[1])
     loads = [
-        load_w,
+        load_w, load_a,
         pltpu.make_async_copy(row_hbm, row_ir, loc.at[2]),
         pltpu.make_async_copy(col_hbm, col_ir, loc.at[3]),
     ]
-    load_a.start()
     for load in loads:
         load.start()
     barrier = pltpu.get_barrier_semaphore()
@@ -76,7 +75,8 @@
     def z_copy(r, s, d, behind):
         sign = 1 if s == 0 else -1
         block = ag.at[lax.rem(z - sign * behind + NZ, NZ), z_rows(r, s, d)]
-        return remote(block, block, sent.at[0], zr.at[r, d - 1] if d < 4 else pb.at[r], dev(dz=sign))
+        src = amp.at[z_rows(r, s, d)] if d == 1 else block
+        return remote(src, block, sent.at[0], zr.at[r, d - 1] if d < 4 else pb.at[r], dev(dz=sign))
 
     def cross_copy(r, s, behind):
         sign = 1 if s == 0 else -1
@@ -102,7 +102,7 @@
         origin = lax.rem(z + far + NZ, NZ)
         rows = pl.ds(starts[r], chunks[r])
         return remote(
-            ag.at[origin, rows], asib.at[lax.div(origin, 2), rows], sent.at[1], (pa if far else pb).at[r], dev(flip=True)
+            ag.at[origin, rows] if far else amp.at[rows], asib.at[lax.div(origin, 2), rows], sent.at[1], (pa if far else pb).at[r], dev(flip=True)
         )
 
     def give(r, d):
@@ -227,7 +227,6 @@
             for s in (0, 1):
                 wb[0, s, :, cols] = (wb[0, s, :, cols].astype(jnp.float32) * keep).astype(jnp.bfloat16)
 
-    load_a.wait()
     pl.semaphore_wait(barrier, len(partners))
 
     def perform(steps):
@@ -297,8 +296,8 @@
     ("wf", 0), ("zf", 0, 2), ("zf", 1, 2), ("zf", 2, 1), ("ws", 0), ("ws", 1), ("zf", 0, 3), ("zf", 3, 1),
     ("zf", 1, 3), ("wf", 1), ("zf", 2, 2), ("pk", 0, 0), ("mm", 0, 0, 1), ("mm", 0, 0, 0), ("pk", 0, 1),
     ("mm", 0, 1, 1), ("zf", 3, 2), ("mm", 0, 1, 0), ("ws", 2), ("mm", 0, 0, 2), ("mm", 0, 1, 2), ("ra", 0, 0, 1),
-    ("wf", 2), ("zf", 2, 3), ("ra", 0, 0, 0), ("ra", 0, 1, 1), ("ra", 0, 1, 0), ("zf", 3, 3), ("ra", 0, 0, 2),
-    ("ra", 0, 1, 2), ("ws", 3), ("mm", 0, 0, 3), ("mm", 0, 1, 3), ("pk", 1, 0), ("pk", 1, 1), ("mm", 1, 0, 3),
+    ("wf", 2), ("zf", 2, 3), ("ra", 0, 0, 0), ("ra", 0, 1, 1), ("ra", 0, 1, 0), ("zf", 3, 3), ("ws", 3),
+    ("mm", 0, 0, 3), ("mm", 0, 1, 3), ("ra", 0, 0, 2), ("ra", 0, 1, 2), ("pk", 1, 0), ("pk", 1, 1), ("mm", 1, 0, 3),
     ("mm", 1, 1, 3), ("mm", 1, 0, 1), ("mm", 1, 1, 1), ("mm", 1, 0, 2), ("mm", 1, 1, 2), ("fi", 0, 0, 1),
     ("fi", 0, 1, 1), ("ra", 0, 0, 3), ("ra", 0, 1, 3), ("fi", 0, 0, 2), ("fi", 0, 1, 2), ("ra", 1, 0, 3),
     ("ra", 1, 1, 3), ("fi", 0, 0, 0), ("fi", 0, 1, 0), ("ra", 1, 0, 1), ("ra", 1, 1, 1), ("mm", 1, 0, 0),

time: 48.2 us -> 48.1 us (level)
  no operation moved by 1% of the time
where the time goes in v6:
time: 48.1 us; the launch traced here: 47.7 us
  Pallas kernels  46.9 us (98%)
  local copies, waits for them, and re-layouts  0.8 us (2%)
    pallas_call x1, Pallas kernels, on_device(): pl.pallas_call(kernel, out_shape=jax.ShapeDtypeStruct((1024, 256), bf16),...  46.9 us

profile of v6, /device:TPU:32, one launch (start us, length us, event | category | flops | bytes accessed | tf_op | source)
XLA Modules:
  0.0 47.7 jit_solution(7578970854303456881)
XLA Ops:
  0.0 46.9 %ladder.1 = bf16[1024,256]{1,0:T(8,128)(2,1)S(1)} custom-call(bf16[256,512]{1,0:T(8,128)(2,1)} %amp.1, bf16[2,256,512]{2,1,0:T(8,128)(2,1)} %integ.1, s32[1,2]{1,0:T(1,128)} %row_hbm.1, s32[2,2]{1,0:T(2,128)} %col_hbm.1), custom_call_target="tpu_custom_call" | custom-call | flops 2147483648 | bytes 2097152 | tf_op jit(solution)/shard_map/ladder/pallas_call | solution.py:313
  46.9 0.8 %copy.6 = bf16[1024,256]{1,0:T(8,128)(2,1)} copy(bf16[1024,256]{1,0:T(8,128)(2,1)S(1)} %ladder.1) | data formatting | bytes 1048576

commit v7 on v5

--- a/solution.py
+++ b/solution.py
@@ -139,7 +139,7 @@
         return {1: (-1, 1), 2: (1, -1), 3: (2, 2)}[g][h]
 
     def o_copy(b, g, h, to):
-        cols = pl.ds(128 * h, 128)
+        cols = pl.ds(128 * h, 128) if g < 3 else pl.ds(0, 256)
         dst = out.at[pl.ds(pl.multiple_of(y * 256 + 128 * b, 128), 128), cols]
         return remote(res.at[pl.ds(128 * (4 * b + g), 128), cols], dst, sent.at[6], orr, to)
 
@@ -213,7 +213,7 @@
                 else:
                     res[pl.ds(128 * (4 * b + g) + 64 * s, 64)] = total
             if g > 0:
-                for h in (0, 1):
+                for h in (0, 1) if g < 3 else (0,):
                     o_copy(b, g, h, dev(dy=owner(g, h))).start()
         pl.when(is_target(e))(act)
 

time: 48.2 us -> 48.2 us (level)
  no operation moved by 1% of the time
where the time goes in v7:
time: 48.2 us; the launch traced here: 48.1 us
  Pallas kernels  47.3 us (98%)
  local copies, waits for them, and re-layouts  0.8 us (2%)
    pallas_call x1, Pallas kernels, on_device(): pl.pallas_call(kernel, out_shape=jax.ShapeDtypeStruct((1024, 256), bf16),...  47.3 us

profile of v7, /device:TPU:32, one launch (start us, length us, event | category | flops | bytes accessed | tf_op | source)
XLA Modules:
  0.0 48.1 jit_solution(2735227801645738273)
XLA Ops:
  0.0 47.3 %ladder.1 = bf16[1024,256]{1,0:T(8,128)(2,1)S(1)} custom-call(bf16[256,512]{1,0:T(8,128)(2,1)} %amp.1, bf16[2,256,512]{2,1,0:T(8,128)(2,1)} %integ.1, s32[1,2]{1,0:T(1,128)} %row_hbm.1, s32[2,2]{1,0:T(2,128)} %col_hbm.1), custom_call_target="tpu_custom_call" | custom-call | flops 2147483648 | bytes 2097152 | tf_op jit(solution)/shard_map/ladder/pallas_call | solution.py:314
  47.3 0.8 %copy.6 = bf16[1024,256]{1,0:T(8,128)(2,1)} copy(bf16[1024,256]{1,0:T(8,128)(2,1)S(1)} %ladder.1) | data formatting | bytes 1048576
